TPU v7x, 128 devices: a whole 4x4x4 slice. The times are simulated.
128 devices in a mesh: tok: 8 (over z, core), lat: 16 (over y, x).
Axes of the slice: x: 4, y: 4, z: 4, core: 2. Of those that a mesh axis runs over, the one named last changes fastest.
Arguments:
- activations: bfloat16 [2048, 2, 8192], P('lat', None, 'tok'), may hold values from -6 to 6
- enc_weight: bfloat16 [64, 2, 8192, 256], P('lat', None, 'tok'), may hold values from -0.046875 to 0.046875
- enc_bias: float32 [64, 256], P('lat'), may hold values from -3 to 3
- dec_weight: bfloat16 [64, 256, 2, 8192], P('lat', None, None, 'tok'), may hold values from -0.09375 to 0.09375
- dec_bias: float32 [2, 8192], P(None, 'tok'), may hold values from -3 to 3
- active: int32 [16, 16], replicated, may hold values from 0 to 63, all different within a row; in each aligned block of 16 rows (0 to 15, 16 to 31, ...) at most 8 rows name the same one
Outputs:
- grad_enc: bfloat16 [64, 2, 8192, 256], P('lat', None, 'tok')
- grad_enc_bias: float32 [64, 256], P('lat')
- grad_dec: bfloat16 [64, 256, 2, 8192], P('lat', None, None, 'tok')
- grad_dec_bias: float32 [2, 8192], P(None, 'tok')
Inputs may be any that keep to these rules, and one draw needn't show every extreme that they name: `active`: each row lists 16 different block ids; every block id appears in some row; no block id appears in more than 8 rows, and some block id appears in exactly 8 rows.
All inputs are finite; a program needn't handle non-finite values.
Results may differ from a plain program's by a relative error of at most 0.02.
Values may be sent and summed in bfloat16 or wider, within the bound.
A program may use at most 192 MiB of HBM per device.

v0:
```python
import math
import jax
import jax.numpy as jnp
from jax import lax
from jax.sharding import PartitionSpec as P

MOST = 8
TILE = 128
SPARSITY = 0.25
NORM_EPSILON = 1e-06


def slot_lists(active, first_block, block_count):
    tile_count = active.shape[0]
    block_ids = first_block + jnp.arange(block_count, dtype=jnp.int32)
    is_active = jnp.any(active[:, :, None] == block_ids[None, None, :], axis=1).astype(jnp.int32)
    rank_count = jnp.cumsum(is_active, axis=0)
    wanted = jnp.arange(MOST, dtype=jnp.int32) + 1
    picked = (is_active[:, :, None] == 1) & (rank_count[:, :, None] == wanted[None, None, :])
    tile_ids = jnp.arange(tile_count, dtype=jnp.int32)
    slot_tile = jnp.sum(jnp.where(picked, tile_ids[:, None, None], 0), axis=0)
    live_slot = jnp.any(picked, axis=0)
    return (slot_tile, live_slot)


def on_device(activations, enc_weight, enc_bias, dec_weight, dec_bias, active):
    slab_count = enc_weight.shape[0]
    tile_count = active.shape[0]
    tile_rows = activations.shape[0]
    models = activations.shape[1]
    feat_width = activations.shape[2]
    loss_scale = 1.0 / math.sqrt(MOST * TILE)
    first_block = lax.axis_index("lat") * slab_count
    slot_tile, live_slot = slot_lists(active, first_block, slab_count)
    live_mask = live_slot[:, :, None, None]
    gathered = lax.all_gather(activations, "lat", axis=0, tiled=True)
    tile_acts = gathered.reshape(tile_count, tile_rows, models, feat_width)
    chosen = tile_acts[slot_tile]
    pre_part = jnp.einsum(
        "smrad,sadj->smrj", chosen, enc_weight, preferred_element_type=jnp.float32
    )
    pre_act = lax.psum(pre_part, "tok") + enc_bias[:, None, None, :]
    features = jnp.where(live_mask, jnp.maximum(pre_act, 0.0), 0.0).astype(jnp.bfloat16)
    product = jnp.einsum(
        "smrj,sjad->smrad", features, dec_weight, preferred_element_type=jnp.float32
    )
    partial_value = (
        jnp.zeros((tile_count, tile_rows, models, feat_width), jnp.float32)
        .at[slot_tile]
        .add(product)
    )
    rounded = lax.optimization_barrier(partial_value.astype(jnp.bfloat16)).astype(jnp.float32)
    rounded = rounded.reshape(tile_count * tile_rows, models, feat_width)
    recon_mine = (
        lax.psum_scatter(
            rounded.astype(jnp.bfloat16), "lat", scatter_dimension=0, tiled=True
        ).astype(jnp.float32)
        + dec_bias[None, :, :]
    )
    error_mine = (recon_mine - activations.astype(jnp.float32)).astype(jnp.bfloat16)
    error_all = lax.all_gather(error_mine, "lat", axis=0, tiled=True)
    tile_err = error_all.reshape(tile_count, tile_rows, models, feat_width)
    err_chosen = tile_err[slot_tile]
    grad_part = jnp.einsum(
        "smrad,sjad->smrj", err_chosen, dec_weight, preferred_element_type=jnp.float32
    )
    dec_wide = dec_weight.astype(jnp.float32)
    squares = jnp.sum(jnp.square(dec_wide), axis=3)
    grad_sum, square_sum = (
        lax.psum(grad_part.astype(jnp.bfloat16), "tok").astype(jnp.float32),
        lax.psum(squares.astype(jnp.bfloat16), "tok").astype(jnp.float32),
    )
    dec_norms = jnp.sqrt(square_sum + NORM_EPSILON)
    feat_grad = loss_scale * (grad_sum + SPARSITY * jnp.sum(dec_norms, axis=2)[:, None, None, :])
    pre_grad = jnp.where(features > 0, feat_grad, 0.0).astype(jnp.bfloat16)
    grad_enc = jnp.einsum(
        "smrad,smrj->sadj", chosen, pre_grad, preferred_element_type=jnp.float32
    ).astype(jnp.bfloat16)
    grad_enc_bias = jnp.sum(pre_grad.astype(jnp.float32), axis=(1, 2))
    feat_total = jnp.sum(features.astype(jnp.float32), axis=(1, 2))
    recon_term = jnp.einsum(
        "smrj,smrad->sjad", features, err_chosen, preferred_element_type=jnp.float32
    )
    norm_term = SPARSITY * feat_total[:, :, None, None] * dec_wide / dec_norms[:, :, :, None]
    grad_dec = (loss_scale * (recon_term + norm_term)).astype(jnp.bfloat16)
    grad_dec_bias = loss_scale * jnp.sum(error_all.astype(jnp.float32), axis=0)
    return (grad_enc, grad_enc_bias, grad_dec, grad_dec_bias)


def solution(mesh):
    placed = (
        P("lat", None, "tok"),
        P("lat", None, "tok", None),
        P("lat", None),
        P("lat", None, None, "tok"),
        P(None, "tok"),
        P(),
    )
    return jax.shard_map(
        on_device,
        mesh=mesh,
        in_specs=placed,
        out_specs=(
            P("lat", None, "tok", None),
            P("lat", None),
            P("lat", None, None, "tok"),
            P(None, "tok"),
        ),
        check_vma=False,
    )
```

profile of v0, /device:TPU:0, one launch (start us, length us, event | category | flops | bytes accessed | tf_op | source)
XLA Modules:
  0.0 585.7 jit_solution(5982257089558291725)
XLA Ops:
  7.2 2.0 copy.46
  9.3 0.9 compare_reduce_fusion
  10.2 0.1 copy.47
  10.4 0.2 select_reduce_fusion
  10.7 73.1 %all-gather.3.cloned.1.call-done = bf16[2048,2,1024]{2,0,1:T(8,128)(2,1)} async-done(((bf16[128,2,1024]{2,0,1:T(8,128)(2,1)}), bf16[2048,2,1024]{2,0,1:T(8,128)(2,1)}) %all-gather.3.cloned.1.call-update) | async-done | bytes 8388624 | tf_op jit(solution)/shard_map/all_gather | solution.py:36
  83.8 8.2 %copy.49 = bf16[16,128,2,1024]{3,1,2,0:T(8,128)(2,1)} copy(bf16[16,128,2,1024]{3,1,0,2:T(8,128)(2,1)} %bitcast.69) | data formatting | bytes 16777216 | tf_op jit(solution)/shard_map/reshape | solution.py:37
  92.0 10.6 %gather_fusion = bf16[32,128,2,1024]{3,1,2,0:T(8,128)(2,1)} fusion(bf16[16,128,2,1024]{3,1,2,0:T(8,128)(2,1)} %copy.49, s32[1024]{0:T(1024)S(1)} %pad_clamp_fusion), kind=kCustom, calls=%fused_computation | custom fusion | bytes 33554560 | tf_op jit(solution)/shard_map/gather | solution.py:38
  102.6 13.5 %fusion.11 = f32[4,8,128,256]{3,2,1,0:T(8,128)} fusion(bf16[4,8,128,2,1024]{4,2,3,1,0:T(8,128)(2,1)} %bitcast.65, bf16[4,2,1024,256]{3,2,1,0:T(8,128)(2,1)} %param.7), kind=kOutput, calls=%fused_computation.23 | convolution fusion | flops 4294967296 | bytes 25165824 | tf_op jit(solution)/shard_map/smrad,sadj->smrj/dot_general | solution.py:39
  116.1 0.2 reduce-scatter.2.cloned.1.call-start
  116.4 0.2 fusion.19
  116.6 72.3 %all-reduce.3.cloned.1.call-done = f32[4,8,128,256]{3,2,1,0:T(8,128)} async-done(((f32[4,8,128,256]{3,2,1,0:T(8,128)}), f32[4,8,128,256]{3,2,1,0:T(8,128)}) %all-reduce.3.cloned.1.call-update) | async-done | bytes 4194320 | tf_op jit(solution)/shard_map/psum | solution.py:42
  188.9 3.1 select_convert_fusion.1
  192.0 0.4 copy-done
  192.3 13.1 %fusion.9 = f32[4,8,128,2,1024]{4,2,3,1,0:T(8,128)} fusion(bf16[4,256,2,1024,1]{3,2,1,0,4:T(2,128)(2,1)S(1)} %bitcast.64, bf16[4,8,128,256]{3,2,1,0:T(8,128)(2,1)S(1)} %select_convert_fusion.1), kind=kOutput, calls=%fused_computation.21 | convolution fusion | flops 4294967296 | bytes 39845888 | tf_op jit(solution)/shard_map/smrj,sjad->smrad/dot_general | solution.py:44
  205.4 7.8 %broadcast_in_dim.28 = f32[16,128,2,1024]{3,1,2,0:T(8,128)} broadcast(f32[]{:T(128)} %constant.17.clone.1), dimensions={} | broadcast | bytes 16777220 | tf_op jit(solution)/shard_map/broadcast_in_dim | solution.py:48
  213.3 65.6 %scatter_fusion = f32[16,128,2,1024]{3,1,2,0:T(8,128)} fusion(f32[16,128,2,1024]{3,1,2,0:T(8,128)} %broadcast_in_dim.28, s32[32]{0:T(128)S(1)} %reshape.64, f32[32,128,2,1024]{3,1,2,0:T(8,128)} %bitcast.60), kind=kCustom, calls=%fused_computation.2 | custom fusion | flops 8388608 | bytes 100663424 | tf_op jit(solution)/shard_map/scatter-add | solution.py:50
  278.9 9.1 %convert_element_type.66 = bf16[16,128,2,1024]{3,1,2,0:T(8,128)(2,1)} convert(f32[16,128,2,1024]{3,1,2,0:T(8,128)} %scatter_fusion) | non-fusion elementwise | flops 4194304 | bytes 25165824 | tf_op jit(solution)/shard_map/convert_element_type | solution.py:52
  288.0 8.2 %copy.51 = bf16[16,128,2,1024]{3,1,0,2:T(8,128)(2,1)} copy(bf16[16,128,2,1024]{3,1,2,0:T(8,128)(2,1)} %convert_element_type.66) | data formatting | bytes 16777216 | tf_op jit(solution)/shard_map/optimization_barrier | solution.py:52
  296.2 84.8 %reduce-scatter.2.cloned.1.call-done = bf16[128,2,1024]{2,0,1:T(8,128)(2,1)} async-done(((bf16[2048,2,1024]{2,0,1:T(8,128)(2,1)}), bf16[128,2,1024]{2,0,1:T(8,128)(2,1)}) %reduce-scatter.2.cloned.1.call-update) | async-done | bytes 524304 | tf_op jit(solution)/shard_map/reduce_scatter | solution.py:55
  381.1 2.1 subtract_convert_fusion
  383.2 3.4 fusion
  386.6 13.9 %psum.23 = bf16[4,256,2]{1,2,0:T(2,128)(2,1)S(1)} all-reduce(bf16[4,256,2]{1,2,0:T(2,128)(2,1)S(1)} %fusion), channel_id=1, replica_groups=mesh['tok'=8,'lat'=16] {'tok'}, use_global_device_ids=true, to_apply=%region_9.10 | all-reduce | flops 2048 | bytes 8192 | tf_op jit(solution)/shard_map/psum | solution.py:71
  400.5 53.2 %all-gather.5.cloned.1.call-done = bf16[2048,2,1024]{2,0,1:T(8,128)(2,1)} async-done(((bf16[128,2,1024]{2,0,1:T(8,128)(2,1)}), bf16[2048,2,1024]{2,0,1:T(8,128)(2,1)}) %all-gather.5.cloned.1.call-update) | async-done | bytes 8388624 | tf_op jit(solution)/shard_map/all_gather | solution.py:61
  453.7 10.6 %gather_fusion.1 = bf16[32,128,2,1024]{3,1,2,0:T(8,128)(2,1)} fusion(bf16[16,128,2,1024]{3,1,0,2:T(8,128)(2,1)} %bitcast.61, s32[1024]{0:T(1024)S(1)} %pad_clamp_fusion), kind=kCustom, calls=%fused_computation.1 | custom fusion | bytes 33554560 | tf_op jit(solution)/shard_map/gather | solution.py:63
  464.4 12.8 %bitcast_convert_fusion.1 = bf16[4,8,128,256]{3,2,1,0:T(8,128)(2,1)} fusion(bf16[4,8,128,2,1024]{4,2,3,1,0:T(8,128)(2,1)} %bitcast.67, bf16[4,256,2,1024,1]{3,2,1,0,4:T(2,128)(2,1)} %bitcast.63), kind=kOutput, calls=%fused_computation.14 | convolution fusion | flops 4296015872 | bytes 23068672 | tf_op jit(solution)/shard_map/smrad,sjad->smrj/dot_general | solution.py:64
  477.3 5.0 convert_reduce_fusion
  482.3 0.6 broadcast_multiply_fusion
  482.9 60.1 %all-reduce.5.cloned.1.call-done = bf16[4,8,128,256]{3,2,1,0:T(8,128)(2,1)} async-done(((bf16[4,8,128,256]{3,2,1,0:T(8,128)(2,1)}), bf16[4,8,128,256]{3,2,1,0:T(8,128)(2,1)}) %all-reduce.5.cloned.1.call-update) | async-done | bytes 2097168 | tf_op jit(solution)/shard_map/psum | solution.py:70
  543.0 5.1 convert_reduce_fusion.1
  548.0 10.7 %fusion.4 = bf16[4,256,2,1024]{3,1,2,0:T(8,128)(2,1)} fusion(f32[4,256,2]{1,2,0:T(2,128)S(1)} %get-tuple-element.26, f32[4,256]{1,0:T(4,128)S(1)} %broadcast_multiply_fusion.1, bf16[4,256,2,1024]{3,2,1,0:T(2,128)(2,1)S(1)} %copy-done.1, bf16[4,8,128,2,1024]{4,2,3,1,0:T(8,128)(2,1)} %bitcast.68, bf16[4,8,128,256]{3,2,1,0:T(8,128)(2,1)S(1)} %select_convert_fusion.1), kind=kOutput, calls=%fused_computation.11 | convolution fusion | flops 4307550208 | bytes 27275264 | tf_op jit(solution)/shard_map/smrj,smrad->sjad/dot_general | solution.py:81
  558.7 8.7 %copy.58 = bf16[4,256,2,1024]{3,2,1,0:T(2,128)(2,1)} copy(bf16[4,256,2,1024]{3,1,2,0:T(8,128)(2,1)} %fusion.4) | data formatting | bytes 8388608
  567.4 11.8 %bitcast_convert_fusion = bf16[4,2,1024,256]{3,2,1,0:T(8,128)(2,1)} fusion(bf16[4,8,128,2,1024]{4,2,3,1,0:T(8,128)(2,1)} %bitcast.66, bf16[4,8,128,256]{3,2,1,0:T(8,128)(2,1)S(1)} %copy-done.2, bf16[4,8,128,256]{3,2,1,0:T(8,128)(2,1)S(1)} %select_convert_fusion.1, f32[4,256]{1,0:T(4,128)S(1)} %broadcast_multiply_fusion.2), kind=kOutput, calls=%fused_computation.10 | convolution fusion | flops 4303355904 | bytes 25169920 | tf_op jit(solution)/shard_map/smrad,smrj->sadj/dot_general | solution.py:76
  (31 shorter events, 0.5 us)
Async XLA Ops:
  7.2 76.7 %all-gather.3.cloned.1.call-start = ((), (), s32[]{:S(2)}) async-start(), calls=%async_computation.1 | async-start | bytes 8912896 | tf_op jit(solution)/shard_map/all_gather | solution.py:36
  9.2 179.7 %all-reduce.3.cloned.1.call-start = ((), (), s32[]{:S(2)}) async-start(), calls=%async_computation.2 | async-start | bytes 8388608 | tf_op jit(solution)/shard_map/psum | solution.py:42
  116.1 72.8 %copy-start.4 = (f32[4,256]{1,0:T(4,128)S(1)}, f32[4,256]{1,0:T(4,128)}, u32[]{:S(2)}) copy-start(f32[4,256]{1,0:T(4,128)} %param.8) | copy-start | bytes 12292
  116.1 265.0 %reduce-scatter.2.cloned.1.call-start = ((), (), s32[]{:S(2)}) async-start(), calls=%async_computation.3 | async-start | bytes 8912896 | tf_op jit(solution)/shard_map/reduce_scatter | solution.py:55
  188.9 3.4 copy-start
  296.2 84.9 %copy-start.3 = (bf16[128,2,1024]{2,1,0:T(2,128)(2,1)S(1)}, bf16[128,2,1024]{2,1,0:T(2,128)(2,1)}, u32[]{:S(2)}) copy-start(bf16[128,2,1024]{2,1,0:T(2,128)(2,1)} %param.6) | copy-start | bytes 1572868
  296.2 84.9 %copy-start.5 = (f32[2,1024]{1,0:T(2,128)S(1)}, f32[2,1024]{1,0:T(2,128)}, u32[]{:S(2)}) copy-start(f32[2,1024]{1,0:T(2,128)} %param.10) | copy-start | bytes 24580
  296.2 157.5 %all-gather.5.cloned.1.call-start = ((), (), s32[]{:S(2)}) async-start(), calls=%async_computation.4 | async-start | bytes 8912896 | tf_op jit(solution)/shard_map/all_gather | solution.py:61
  383.2 159.8 %all-reduce.5.cloned.1.call-start = ((), (), s32[]{:S(2)}) async-start(), calls=%async_computation.5 | async-start | bytes 4194304 | tf_op jit(solution)/shard_map/psum | solution.py:70
  543.0 5.1 copy-start.1
  558.7 8.7 %copy-start.2 = (bf16[4,8,128,256]{3,2,1,0:T(8,128)(2,1)S(1)}, bf16[4,8,128,256]{3,2,1,0:T(8,128)(2,1)}, u32[]{:S(2)}) copy-start(bf16[4,8,128,256]{3,2,1,0:T(8,128)(2,1)} %all-reduce.5.cloned.1.call-done) | copy-start | bytes 6291460
Sparse Core Ops, SparseCore 0:
  10.7 73.0 all-gather.2
  116.2 72.5 all-reduce.2
  296.3 84.7 reduce-scatter.1
  383.7 70.0 all-gather.4
  477.3 65.6 all-reduce.4
where the time goes:
time: 586 us
  waiting for transfers between devices  344 us (59%)
  other arithmetic  95.3 us (16%)
  matrix products  61.8 us (11%)
  local copies, waits for them, and re-layouts  56.7 us (10%)
  blocking collectives  13.9 us (2%)
  between operations  13.8 us (2%)
    reduce_scatter x1, waiting for transfers between devices, on_device(): lax.psum_scatter(rounded.astype(jnp.bfloat16), 'lat', scatter_dimension=0...  84.8 us
    all_gather x1, waiting for transfers between devices, on_device(): gathered = lax.all_gather(activations, 'lat', axis=0, tiled=True)  73.1 us
    psum x1, waiting for transfers between devices, on_device(): pre_act = lax.psum(pre_part, 'tok') + enc_bias[:, None, None, :]  72.3 us
    scatter-add x1, other arithmetic, on_device(): partial_value = jnp.zeros((tile_count, tile_rows, models, feat_width), jn...  65.6 us
    psum x1, waiting for transfers between devices, on_device(): lax.psum(grad_part.astype(jnp.bfloat16), 'tok').astype(jnp.float32)  60.1 us
    all_gather x1, waiting for transfers between devices, on_device(): error_all = lax.all_gather(error_mine, 'lat', axis=0, tiled=True)  53.2 us
    psum x1, blocking collectives, on_device(): lax.psum(squares.astype(jnp.bfloat16), 'tok').astype(jnp.float32)  13.9 us
    dot_general x1, matrix products, on_device(): jnp.einsum('smrad,sadj->smrj', chosen, enc_weight, preferred_element_type...  13.5 us
  transfers between devices with their start and end apart: 5, of which 5 were waited for; matrix products, arithmetic and copies ran while one was open for 2% of the time, Pallas kernels for 0%

commit v1 on v0

--- a/solution.py
+++ b/solution.py
@@ -33,7 +33,8 @@
     first_block = lax.axis_index("lat") * slab_count
     slot_tile, live_slot = slot_lists(active, first_block, slab_count)
     live_mask = live_slot[:, :, None, None]
-    gathered = lax.all_gather(activations, "lat", axis=0, tiled=True)
+    copies = jnp.concatenate([activations] * lax.axis_size("lat"), axis=0)
+    gathered = lax.all_to_all(copies, "lat", 0, 0, tiled=True)
     tile_acts = gathered.reshape(tile_count, tile_rows, models, feat_width)
     chosen = tile_acts[slot_tile]
     pre_part = jnp.einsum(

time: 586 us -> 681 us (1.16)
  waiting for transfers between devices: 344 us -> 394 us
  local copies, waits for them, and re-layouts: 56.7 us -> 83.1 us
  starting transfers between devices: 0.39 us -> 8.29 us
    all_to_all x0 -> x1, waiting for transfers between devices: none -> 123 us  [on_device(): gathered = lax.all_to_all(copies, 'lat', 0, 0, tiled=True)]
    all_gather x1 -> x0, waiting for transfers between devices: 73.1 us -> none  [on_device(): gathered = lax.all_gather(activations, 'lat', axis=0, tiled=True)]
    unnamed x14 -> x28, local copies, waits for them, and re-layouts: 11 us -> 35 us
    all_to_all x0 -> x1, starting transfers between devices: none -> 7.3 us  [on_device(): gathered = lax.all_to_all(copies, 'lat', 0, 0, tiled=True)]
  transfers between devices with their start and end apart: 5 -> 5, of which waited for: 5 -> 5; matrix products, arithmetic and copies ran while one was open for 2% -> 1% of each run, Pallas kernels for 0% -> 0%
where the time goes in v1:
time: 681 us; the launch traced here: 675 us
  waiting for transfers between devices  394 us (58%)
  other arithmetic  94.5 us (14%)
  local copies, waits for them, and re-layouts  83.1 us (12%)
  matrix products  66.4 us (10%)
  between operations  14.1 us (2%)
  blocking collectives  13.8 us (2%)
  starting transfers between devices  8.29 us (1%)
    all_to_all x1, waiting for transfers between devices, on_device(): gathered = lax.all_to_all(copies, 'lat', 0, 0, tiled=True)  123 us
    reduce_scatter x1, waiting for transfers between devices, on_device(): lax.psum_scatter(rounded.astype(jnp.bfloat16), 'lat', scatter_dimension=0...  84.6 us
    psum x1, waiting for transfers between devices, on_device(): pre_act = lax.psum(pre_part, 'tok') + enc_bias[:, None, None, :]  73.2 us
    scatter-add x1, other arithmetic, on_device(): partial_value = jnp.zeros((tile_count, tile_rows, models, feat_width), jn...  65.6 us
    psum x1, waiting for transfers between devices, on_device(): lax.psum(grad_part.astype(jnp.bfloat16), 'tok').astype(jnp.float32)  60.1 us
    all_gather x1, waiting for transfers between devices, on_device(): error_all = lax.all_gather(error_mine, 'lat', axis=0, tiled=True)  53.4 us
    unnamed x28, local copies, waits for them, and re-layouts  35 us
    dot_general x1, matrix products, on_device(): jnp.einsum('smrj,smrad->sjad', features, err_chosen, preferred_element_ty...  15.2 us
  transfers between devices with their start and end apart: 5, of which 5 were waited for; matrix products, arithmetic and copies ran while one was open for 1% of the time, Pallas kernels for 0%

profile of v1, /device:TPU:0, one launch (start us, length us, event | category | flops | bytes accessed | tf_op | source)
XLA Modules:
  0.0 674.5 jit_solution(6979550592272206515)
XLA Ops:
  7.2 2.3 constant_dynamic-update-slice_fusion.15
  9.5 2.3 constant_dynamic-update-slice_fusion.14
  11.8 2.2 constant_dynamic-update-slice_fusion.13
  14.0 2.2 constant_dynamic-update-slice_fusion.12
  16.1 2.2 constant_dynamic-update-slice_fusion.11
  18.4 2.2 constant_dynamic-update-slice_fusion.10
  20.6 2.2 constant_dynamic-update-slice_fusion.9
  22.8 2.2 constant_dynamic-update-slice_fusion.8
  34.3 7.3 %all-to-all-start = ((bf16[2048,2,1024]{2,1,0:T(2,128)(2,1)}), bf16[2048,2,1024]{2,1,0:T(2,128)(2,1)}, u32[]{:S(2)}, u32[]{:S(2)}) async-start(bf16[2048,2,1024]{2,1,0:T(2,128)(2,1)} %constant_dynamic-update-slice_fusion), calls=%async_computation | async-start | bytes 16777216 | tf_op jit(solution)/shard_map/all_to_all | solution.py:37
  42.8 122.9 %all-to-all-done = bf16[2048,2,1024]{2,1,0:T(2,128)(2,1)} async-done(((bf16[2048,2,1024]{2,1,0:T(2,128)(2,1)}), bf16[2048,2,1024]{2,1,0:T(2,128)(2,1)}, u32[]{:S(2)}, u32[]{:S(2)}) %all-to-all-start) | async-done | bytes 8388640 | tf_op jit(solution)/shard_map/all_to_all | solution.py:37
  165.7 9.4 %copy.75 = bf16[16,128,2,1024]{3,1,2,0:T(8,128)(2,1)} copy(bf16[16,128,2,1024]{3,2,1,0:T(2,128)(2,1)} %bitcast) | data formatting | bytes 16777216 | tf_op jit(solution)/shard_map/reshape | solution.py:38
  175.1 10.6 %gather_fusion = bf16[32,128,2,1024]{3,1,2,0:T(8,128)(2,1)} fusion(bf16[16,128,2,1024]{3,1,2,0:T(8,128)(2,1)} %copy.75, s32[1024]{0:T(1024)S(1)} %pad_clamp_fusion), kind=kCustom, calls=%fused_computation | custom fusion | bytes 33554560 | tf_op jit(solution)/shard_map/gather | solution.py:39
  185.7 13.5 %fusion.11 = f32[4,8,128,256]{3,2,1,0:T(8,128)} fusion(bf16[4,8,128,2,1024]{4,2,3,1,0:T(8,128)(2,1)} %bitcast.65, bf16[4,2,1024,256]{3,2,1,0:T(8,128)(2,1)} %param.7), kind=kOutput, calls=%fused_computation.23 | convolution fusion | flops 4294967296 | bytes 25165824 | tf_op jit(solution)/shard_map/smrad,sadj->smrj/dot_general | solution.py:40
  200.0 73.2 %all-reduce.3.cloned.1.call-done = f32[4,8,128,256]{3,2,1,0:T(8,128)} async-done(((f32[4,8,128,256]{3,2,1,0:T(8,128)}), f32[4,8,128,256]{3,2,1,0:T(8,128)}) %all-reduce.3.cloned.1.call-update) | async-done | bytes 4194320 | tf_op jit(solution)/shard_map/psum | solution.py:43
  273.2 3.1 select_convert_fusion.1
  276.7 13.1 %fusion.9 = f32[4,8,128,2,1024]{4,2,3,1,0:T(8,128)} fusion(bf16[4,256,2,1024,1]{3,2,1,0,4:T(2,128)(2,1)S(1)} %bitcast.64, bf16[4,8,128,256]{3,2,1,0:T(8,128)(2,1)S(1)} %select_convert_fusion.1), kind=kOutput, calls=%fused_computation.21 | convolution fusion | flops 4294967296 | bytes 39845888 | tf_op jit(solution)/shard_map/smrj,sjad->smrad/dot_general | solution.py:45
  289.8 7.8 %broadcast_in_dim.28 = f32[16,128,2,1024]{3,1,2,0:T(8,128)} broadcast(f32[]{:T(128)} %constant.17.clone.1), dimensions={} | broadcast | bytes 16777220 | tf_op jit(solution)/shard_map/broadcast_in_dim | solution.py:49
  297.6 65.6 %scatter_fusion = f32[16,128,2,1024]{3,1,2,0:T(8,128)} fusion(f32[16,128,2,1024]{3,1,2,0:T(8,128)} %broadcast_in_dim.28, s32[32]{0:T(128)S(1)} %reshape.64, f32[32,128,2,1024]{3,1,2,0:T(8,128)} %bitcast.60), kind=kCustom, calls=%fused_computation.2 | custom fusion | flops 8388608 | bytes 100663424 | tf_op jit(solution)/shard_map/scatter-add | solution.py:51
  363.3 9.1 %convert_element_type.66 = bf16[16,128,2,1024]{3,1,2,0:T(8,128)(2,1)} convert(f32[16,128,2,1024]{3,1,2,0:T(8,128)} %scatter_fusion) | non-fusion elementwise | flops 4194304 | bytes 25165824 | tf_op jit(solution)/shard_map/convert_element_type | solution.py:53
  372.4 8.2 %copy.77 = bf16[16,128,2,1024]{3,1,0,2:T(8,128)(2,1)} copy(bf16[16,128,2,1024]{3,1,2,0:T(8,128)(2,1)} %convert_element_type.66) | data formatting | bytes 16777216 | tf_op jit(solution)/shard_map/optimization_barrier | solution.py:53
  380.6 84.6 %reduce-scatter.2.cloned.1.call-done = bf16[128,2,1024]{2,0,1:T(8,128)(2,1)} async-done(((bf16[2048,2,1024]{2,0,1:T(8,128)(2,1)}), bf16[128,2,1024]{2,0,1:T(8,128)(2,1)}) %reduce-scatter.2.cloned.1.call-update) | async-done | bytes 524304 | tf_op jit(solution)/shard_map/reduce_scatter | solution.py:56
  467.3 3.4 fusion
  470.7 13.8 %psum.23 = bf16[4,256,2]{1,2,0:T(2,128)(2,1)S(1)} all-reduce(bf16[4,256,2]{1,2,0:T(2,128)(2,1)S(1)} %fusion), channel_id=1, replica_groups=mesh['tok'=8,'lat'=16] {'tok'}, use_global_device_ids=true, to_apply=%region_9.10 | all-reduce | flops 2048 | bytes 8192 | tf_op jit(solution)/shard_map/psum | solution.py:72
  484.5 53.4 %all-gather.2.cloned.1.call-done = bf16[2048,2,1024]{2,0,1:T(8,128)(2,1)} async-done(((bf16[128,2,1024]{2,0,1:T(8,128)(2,1)}), bf16[2048,2,1024]{2,0,1:T(8,128)(2,1)}) %all-gather.2.cloned.1.call-update) | async-done | bytes 8388624 | tf_op jit(solution)/shard_map/all_gather | solution.py:62
  538.0 10.6 %gather_fusion.1 = bf16[32,128,2,1024]{3,1,2,0:T(8,128)(2,1)} fusion(bf16[16,128,2,1024]{3,1,0,2:T(8,128)(2,1)} %bitcast.61, s32[1024]{0:T(1024)S(1)} %pad_clamp_fusion), kind=kCustom, calls=%fused_computation.1 | custom fusion | bytes 33554560 | tf_op jit(solution)/shard_map/gather | solution.py:64
  548.6 12.8 %bitcast_convert_fusion.1 = bf16[4,8,128,256]{3,2,1,0:T(8,128)(2,1)} fusion(bf16[4,8,128,2,1024]{4,2,3,1,0:T(8,128)(2,1)} %bitcast.67, bf16[4,256,2,1024,1]{3,2,1,0,4:T(2,128)(2,1)} %bitcast.63), kind=kOutput, calls=%fused_computation.14 | convolution fusion | flops 4296015872 | bytes 23068672 | tf_op jit(solution)/shard_map/smrad,sjad->smrj/dot_general | solution.py:65
  561.5 5.0 convert_reduce_fusion
  567.1 60.1 %all-reduce.5.cloned.1.call-done = bf16[4,8,128,256]{3,2,1,0:T(8,128)(2,1)} async-done(((bf16[4,8,128,256]{3,2,1,0:T(8,128)(2,1)}), bf16[4,8,128,256]{3,2,1,0:T(8,128)(2,1)}) %all-reduce.5.cloned.1.call-update) | async-done | bytes 2097168 | tf_op jit(solution)/shard_map/psum | solution.py:71
  627.2 4.9 convert_reduce_fusion.1
  632.1 15.2 %fusion.4 = bf16[4,256,2,1024]{3,1,2,0:T(8,128)(2,1)} fusion(f32[4,256,2]{1,2,0:T(2,128)S(1)} %get-tuple-element.30, f32[4,256]{1,0:T(4,128)S(1)} %broadcast_multiply_fusion.1, bf16[4,256,2,1024]{3,2,1,0:T(2,128)(2,1)} %param.9, bf16[4,8,128,2,1024]{4,2,3,1,0:T(8,128)(2,1)} %bitcast.68, bf16[4,8,128,256]{3,2,1,0:T(8,128)(2,1)S(1)} %select_convert_fusion.1), kind=kOutput, calls=%fused_computation.11 | convolution fusion | flops 4307550208 | bytes 27275264 | tf_op jit(solution)/shard_map/smrj,smrad->sjad/dot_general | solution.py:82
  647.3 8.7 %copy.84 = bf16[4,256,2,1024]{3,2,1,0:T(2,128)(2,1)} copy(bf16[4,256,2,1024]{3,1,2,0:T(8,128)(2,1)} %fusion.4) | data formatting | bytes 8388608
  656.0 11.8 %bitcast_convert_fusion = bf16[4,2,1024,256]{3,2,1,0:T(8,128)(2,1)} fusion(bf16[4,8,128,2,1024]{4,2,3,1,0:T(8,128)(2,1)} %bitcast.66, bf16[4,8,128,256]{3,2,1,0:T(8,128)(2,1)S(1)} %copy-done.2, bf16[4,8,128,256]{3,2,1,0:T(8,128)(2,1)S(1)} %select_convert_fusion.1, f32[4,256]{1,0:T(4,128)S(1)} %broadcast_multiply_fusion.2), kind=kOutput, calls=%fused_computation.10 | convolution fusion | flops 4303355904 | bytes 25169920 | tf_op jit(solution)/shard_map/smrad,smrj->sadj/dot_general | solution.py:77
  (45 shorter events, 14.4 us)
Async XLA Ops:
  7.2 17.8 %copy-start = (bf16[128,2,1024]{2,1,0:T(2,128)(2,1)S(1)}, bf16[128,2,1024]{2,1,0:T(2,128)(2,1)}, u32[]{:S(2)}) copy-start(bf16[128,2,1024]{2,1,0:T(2,128)(2,1)} %param.6) | copy-start | bytes 1572868
  34.3 7.7 %copy-start.5 = (s32[16,16]{1,0:T(8,128)S(1)}, s32[16,16]{1,0:T(8,128)}, u32[]{:S(2)}) copy-start(s32[16,16]{1,0:T(8,128)} %param.11) | copy-start | bytes 3076
  34.3 131.3 %all-to-all-start = ((bf16[2048,2,1024]{2,1,0:T(2,128)(2,1)}), bf16[2048,2,1024]{2,1,0:T(2,128)(2,1)}, u32[]{:S(2)}, u32[]{:S(2)}) async-start(bf16[2048,2,1024]{2,1,0:T(2,128)(2,1)} %constant_dynamic-update-slice_fusion), calls=%async_computation | async-start | bytes 16777216 | tf_op jit(solution)/shard_map/all_to_all | solution.py:37
  41.7 231.6 %all-reduce.3.cloned.1.call-start = ((), (), s32[]{:S(2)}) async-start(), calls=%async_computation.2 | async-start | bytes 8388608 | tf_op jit(solution)/shard_map/psum | solution.py:43
  185.7 87.5 %copy-start.3 = (f32[4,256]{1,0:T(4,128)S(1)}, f32[4,256]{1,0:T(4,128)}, u32[]{:S(2)}) copy-start(f32[4,256]{1,0:T(4,128)} %param.8) | copy-start | bytes 12292
  199.2 266.0 %reduce-scatter.2.cloned.1.call-start = ((), (), s32[]{:S(2)}) async-start(), calls=%async_computation.3 | async-start | bytes 8912896 | tf_op jit(solution)/shard_map/reduce_scatter | solution.py:56
  273.2 3.4 copy-start.1
  380.5 84.7 %copy-start.4 = (f32[2,1024]{1,0:T(2,128)S(1)}, f32[2,1024]{1,0:T(2,128)}, u32[]{:S(2)}) copy-start(f32[2,1024]{1,0:T(2,128)} %param.10) | copy-start | bytes 24580
  380.6 157.4 %all-gather.2.cloned.1.call-start = ((), (), s32[]{:S(2)}) async-start(), calls=%async_computation.4 | async-start | bytes 8912896 | tf_op jit(solution)/shard_map/all_gather | solution.py:62
  467.3 159.9 %all-reduce.5.cloned.1.call-start = ((), (), s32[]{:S(2)}) async-start(), calls=%async_computation.5 | async-start | bytes 4194304 | tf_op jit(solution)/shard_map/psum | solution.py:71
  647.3 8.7 %copy-start.2 = (bf16[4,8,128,256]{3,2,1,0:T(8,128)(2,1)S(1)}, bf16[4,8,128,256]{3,2,1,0:T(8,128)(2,1)}, u32[]{:S(2)}) copy-start(bf16[4,8,128,256]{3,2,1,0:T(8,128)(2,1)} %all-reduce.5.cloned.1.call-done) | copy-start | bytes 6291460
Sparse Core Ops, SparseCore 0:
  199.3 73.8 all-reduce.2
  380.7 84.4 reduce-scatter.1
  467.9 69.9 all-gather.1
  561.6 65.6 all-reduce.4
